TPU v7x, 32 devices: a whole 2x2x4 slice. The times are simulated.
32 devices in a mesh: vocab: 8 (over z, y), batch: 4 (over x, core).
Axes of the slice: x: 2, y: 2, z: 4, core: 2. Of those that a mesh axis runs over, the one named last changes fastest.
Arguments:
- early_depth_activity: bfloat16 [16, 4, 8192], P('batch', None, 'vocab')
- deepest_depth_activity: bfloat16 [16, 5, 8192], P('batch', None, 'vocab')
- closing_gain_vector: bfloat16 [8192], replicated, may hold values from 0.5 to 1.5
- common_output_matrix: bfloat16 [8192, 128256], P('batch', 'vocab')
- softness_factor: float32 [16], P('batch'), may hold values from 0.2 to 1
- guessed_symbol_list: int32 [16, 4], P('batch'), may hold values from 0 to 128255
- acceptance_draw_numerators: int32 [16, 4], P('batch'), may hold values from 0 to 16777215
Outputs:
- draft_logprob: float32 [16, 4], P('batch')
- target_logprob: float32 [16, 4], P('batch')
- draft_best: int32 [16, 4], P('batch')
- target_best: int32 [16, 5], P('batch')
- accepted: int32 [16], P('batch')
- next_token: int32 [16], P('batch')
- accepted_total: int32 [], replicated
All inputs are finite; a program needn't handle non-finite values.
Results may differ from a plain program's by a relative error of at most 0.00037.
Values may be sent and summed in bfloat16 or wider, within the bound.
A program may use at most 128 MiB of HBM per device.

v0:
```python
import jax
import jax.numpy as jnp
from jax import lax
from jax.sharding import PartitionSpec as P

epsilon = 1e-05
inverse_range = 1.0 / 16777216.0


def joined(array, axis, combine):
    everything = jax.tree.map(lambda part: lax.all_gather(part, axis), array)
    leading = jax.tree.map(lambda part: part[0], everything)

    def lap(k, so_far):
        return combine(so_far, jax.tree.map(lambda part: part[k], everything))

    return lax.fori_loop(1, lax.axis_size(axis), lap, leading)


def combine_rows(left_part, right_part):
    left_top, left_total, left_index, left_picked = left_part
    right_top, right_total, right_index, right_picked = right_part
    joined_top = jnp.maximum(left_top, right_top)
    joined_total = left_total * jnp.exp(left_top - joined_top) + right_total * jnp.exp(
        right_top - joined_top
    )
    joined_index = jnp.where(
        left_top > right_top,
        left_index,
        jnp.where(right_top > left_top, right_index, jnp.minimum(left_index, right_index)),
    )
    return (joined_top, joined_total, joined_index, left_picked + right_picked)


def on_device(
    early_depth_activity,
    deepest_depth_activity,
    closing_gain_vector,
    common_output_matrix,
    softness_factor,
    guessed_symbol_list,
    acceptance_draw_numerators,
):
    drafts = early_depth_activity.shape[1]
    stacked = jnp.concatenate([early_depth_activity, deepest_depth_activity], 1)
    gathered = lax.all_gather(stacked, "vocab", axis=2, tiled=True)
    widened = gathered.astype(jnp.float32)
    normed = (
        widened
        * lax.rsqrt(jnp.mean(widened * widened, -1, keepdims=True) + epsilon)
        * closing_gain_vector.astype(jnp.float32)
    ).astype(jnp.bfloat16)
    seq_count, row_count, full_width = normed.shape
    flat_count = seq_count * row_count
    col_count = common_output_matrix.shape[1]
    spread = lax.all_to_all(normed, "batch", split_axis=2, concat_axis=0, tiled=True)
    flat_spread = spread.reshape(spread.shape[0] * spread.shape[1], spread.shape[2])
    unnormalized_preference = lax.psum_scatter(
        jnp.dot(flat_spread, common_output_matrix, preferred_element_type=jnp.float32),
        "batch",
        scatter_dimension=0,
        tiled=True,
    )
    row_softness = jnp.broadcast_to(softness_factor[:, None], (seq_count, row_count)).reshape(
        flat_count
    )
    gained_activity = unnormalized_preference / row_softness[:, None]
    offset = lax.axis_index("vocab") * col_count
    columns = offset + lax.broadcasted_iota(jnp.int32, (1, col_count), 1)
    token_ids = jnp.concatenate(
        [guessed_symbol_list, guessed_symbol_list, jnp.full((seq_count, 1), -1, jnp.int32)], 1
    )
    flat_ids = token_ids.reshape(flat_count)
    picked = jnp.sum(jnp.where(columns == flat_ids[:, None], gained_activity, jnp.float32(0.0)), -1)
    local_top = jnp.max(gained_activity, -1)
    local_best = jnp.argmax(gained_activity, -1) + offset
    shifted = jnp.sum(jnp.exp(gained_activity - local_top[:, None]), -1)
    row_top, row_total, index_float, picked = joined(
        (local_top, shifted, local_best.astype(jnp.float32), picked), "vocab", combine_rows
    )
    best_index = index_float.astype(jnp.int32)
    log_norm = row_top + jnp.log(row_total)
    logprob = (picked - log_norm).reshape(seq_count, row_count)
    best_index = best_index.reshape(seq_count, row_count)
    draft_logprob = logprob[:, :drafts]
    target_logprob = logprob[:, drafts : 2 * drafts]
    draft_best = best_index[:, :drafts]
    target_best = best_index[:, drafts:]
    passing = acceptance_draw_numerators.astype(jnp.float32) * inverse_range < jnp.exp(
        target_logprob - draft_logprob
    )
    accepted = jnp.sum(jnp.cumprod(passing.astype(jnp.int32), 1), 1)
    position = lax.broadcasted_iota(jnp.int32, (1, drafts + 1), 1)
    next_token = jnp.sum(jnp.where(position == accepted[:, None], target_best, 0), 1)
    summed = lax.psum(jnp.sum(accepted).astype(jnp.float32), "batch")
    accepted_total = summed.astype(jnp.int32)
    return (
        draft_logprob,
        target_logprob,
        draft_best,
        target_best,
        accepted,
        next_token,
        accepted_total,
    )


def solution(mesh):
    return jax.shard_map(
        on_device,
        mesh=mesh,
        in_specs=(
            P("batch", None, "vocab"),
            P("batch", None, "vocab"),
            P(),
            P("batch", "vocab"),
            P("batch"),
            P("batch", None),
            P("batch", None),
        ),
        out_specs=(
            P("batch", None),
            P("batch", None),
            P("batch", None),
            P("batch", None),
            P("batch"),
            P("batch"),
            P(),
        ),
        check_vma=False,
    )
```

profile of v0, /device:TPU:0, one launch (start us, length us, event | category | flops | bytes accessed | tf_op | source)
XLA Modules:
  0.0 296.5 jit_solution(8542964603200034650)
XLA Ops:
  0.6 0.8 copy.20
  1.4 0.8 pad_maximum_fusion
  2.2 33.2 %all_gather.27 = bf16[4,9,8192]{2,0,1:T(4,128)(2,1)S(1)} all-gather(bf16[4,9,1024]{2,0,1:T(4,128)(2,1)S(1)} %pad_maximum_fusion), channel_id=1, replica_groups=mesh['vocab'=8,'batch'=4] {'vocab'}, dimensions={2}, use_global_device_ids=true | all-gather | bytes 663552 | tf_op jit(solution)/shard_map/all_gather | solution.py:46
  35.5 0.4 fusion.9
  35.9 0.7 convert_element_type.28
  36.6 0.4 fusion.11
  37.0 8.6 %copy.21 = bf16[4,9,8192]{1,0,2:T(4,128)(2,1)} copy(bf16[4,9,8192]{2,0,1:T(4,128)(2,1)S(1)} %fusion.11) | data formatting | bytes 1179648 | tf_op jit(solution)/shard_map/convert_element_type | solution.py:52
  45.6 13.8 %reshape.80 = bf16[4,2,36864]{2,1,0:T(2,128)(2,1)S(1)} reshape(bf16[8192,4,9]{2,1,0:T(4,128)(2,1)} %bitcast.37) | data formatting | bytes 1179648
  59.3 12.1 %all_to_all.15 = bf16[4,2,36864]{2,1,0:T(2,128)(2,1)S(1)} all-to-all(bf16[4,2,36864]{2,1,0:T(2,128)(2,1)S(1)} %reshape.80), channel_id=1, replica_groups=mesh['vocab'=8,'batch'=4] {'batch'}, dimensions={0} | all-to-all | bytes 1179648 | tf_op jit(solution)/shard_map/all_to_all | solution.py:56
  71.4 20.3 %reshape.81 = bf16[8192,4,9]{2,1,0:T(4,128)(2,1)} reshape(bf16[4,2,36864]{2,1,0:T(2,128)(2,1)S(1)} %all_to_all.15) | data formatting | bytes 1179648
  91.8 12.0 %copy.22 = bf16[4,9,4,2048]{3,1,0,2:T(8,128)(2,1)S(1)} copy(bf16[4,9,4,2048]{1,0,3,2:T(4,128)(2,1)} %bitcast.38) | data formatting | bytes 1179648 | tf_op jit(solution)/shard_map/all_to_all | solution.py:56
  103.8 0.3 reshape.43
  104.0 31.5 %fusion.15 = f32[144,16032]{1,0:T(8,128)} fusion(bf16[144,2048]{1,0:T(8,128)(2,1)S(1)} %reshape.43, bf16[2048,16032]{0,1:T(8,128)(2,1)} %param.12), kind=kOutput, calls=%fused_computation.34 | convolution fusion | flops 9456058368 | bytes 75491328 | tf_op jit(solution)/shard_map/dot_general | solution.py:59
  135.6 90.5 %fusion = f32[40,16032]{1,0:T(8,128)S(1)} fusion(f32[144,16032]{1,0:T(8,128)} %fusion.15), kind=kCustom, calls=%all-reduce-scatter | all-reduce-scatter fusion | flops 2565121 | bytes 11800064
  226.1 1.1 slice.36
  227.2 2.2 collective-permute-start
  229.8 0.6 dynamic-slice.8
  231.1 0.6 dynamic-slice
  232.3 12.7 %concatenate.8 = f32[52,16032]{1,0:T(8,128)} concatenate(f32[12,16032]{1,0:T(8,128)} %collective-permute-done, f32[40,16032]{1,0:T(8,128)S(1)} %fusion), dimensions={0} | concatenate | bytes 6669312
  245.0 3.9 %iota_reduce_fusion = (f32[36]{0:T(128)S(1)}, s32[36]{0:T(128)S(1)}) fusion(f32[36]{0:T(128)S(1)} %div.18, f32[52,16032]{1,0:T(8,128)} %concatenate.8, u32[]{:S(6)} %subtract), kind=kLoop, calls=%fused_computation.17 | loop fusion | flops 5771196 | bytes 2309044 | tf_op jit(solution)/shard_map/on_device/reduce | solution.py:76
  248.9 2.9 select_reduce_fusion
  251.8 0.2 dynamic-update-slice
  252.0 0.2 dynamic-update-slice.3
  252.2 0.2 dynamic-update-slice.1
  252.5 0.1 convert_dynamic-update-slice_fusion
  252.5 21.7 %all-reduce.6 = (f32[288]{0:T(512)S(1)}, f32[288]{0:T(512)S(1)}, f32[288]{0:T(512)S(1)}, f32[288]{0:T(512)S(1)}) all-reduce(f32[288]{0:T(512)S(1)} %dynamic-update-slice, f32[288]{0:T(512)S(1)} %dynamic-update-slice.1, f32[288]{0:T(512)S(1)} %convert_dynamic-update-slice_fusion, ...), channel_id=2, replica_groups=mesh['vocab'=8,'batch'=4] {'vocab'}, use_global_device_ids=true, to_apply=%add | all-reduce | flops 1152 | bytes 9216
  274.6 0.3 while.21
  275.0 0.7 fusion.12
  275.7 0.2 reduce_window.9
  275.9 0.7 fusion.13
  277.3 16.1 %psum.7 = f32[]{:T(128)} all-reduce(f32[]{:T(128)S(6)} %convert_element_type.34), channel_id=1, replica_groups=mesh['vocab'=8,'batch'=4] {'batch'}, use_global_device_ids=true, to_apply=%region_11.12 | all-reduce | flops 1 | bytes 8 | tf_op jit(solution)/shard_map/psum | solution.py:95
  294.1 1.3 select_reduce_fusion.1
  (45 shorter events, 1.1 us)
Async XLA Ops:
  135.6 93.9 %copy-start.4 = (f32[4]{0:T(128)S(1)}, f32[4]{0:T(128)}, u32[]{:S(2)}) copy-start(f32[4]{0:T(128)} %param.13) | copy-start | bytes 52
  135.6 94.1 %copy-start.1 = (s32[4,4]{1,0:T(4,128)S(1)}, s32[4,4]{1,0:T(4,128)}, u32[]{:S(2)}) copy-start(s32[4,4]{1,0:T(4,128)} %param.14) | copy-start | bytes 196
  135.6 94.3 %copy-start.5 = (u32[32]{0:T(128)S(1)}, u32[32]{0:T(128)}, u32[]{:S(2)}) copy-start(u32[32]{0:T(128)} %constant.93) | copy-start | bytes 388
  135.6 95.5 %copy-start.6 = (u32[32]{0:T(128)S(1)}, u32[32]{0:T(128)}, u32[]{:S(2)}) copy-start(u32[32]{0:T(128)} %constant.69) | copy-start | bytes 388
  227.2 5.1 %collective-permute-start = (f32[12,16032]{1,0:T(8,128)}, f32[12,16032]{1,0:T(8,128)}, u32[]{:S(2)}, u32[]{:S(2)}) collective-permute-start(f32[12,16032]{1,0:T(8,128)} %slice.36), channel_id=1, source_target_pairs={{0,1},{1,2},{2,3},{4,5},{5,6},{6,7},{8,9},{9,10},{10,11},{12,13},{... | collective-permute-start | bytes 2308616
  245.0 30.0 %copy-start.3 = (s32[4,4]{1,0:T(4,128)S(1)}, s32[4,4]{1,0:T(4,128)}, u32[]{:S(2)}) copy-start(s32[4,4]{1,0:T(4,128)} %param.15) | copy-start | bytes 196
  276.5 18.8 %copy-start.2 = (s32[4]{0:T(128)}, s32[4]{0:T(128)S(1)}, u32[]{:S(2)}) copy-start(s32[4]{0:T(128)S(1)} %get-tuple-element.242) | copy-start | bytes 52
  277.3 18.1 %copy-start = (s32[4,9]{1,0:T(4,128)}, s32[4,9]{1,0:T(4,128)S(1)}, u32[]{:S(2)}) copy-start(s32[4,9]{1,0:T(4,128)S(1)} %reshape.45) | copy-start | bytes 436
where the time goes:
time: 298 us; the launch traced here: 296 us
  blocking collectives  174 us (58%)
  local copies, waits for them, and re-layouts  72.1 us (24%)
  matrix products  31.5 us (11%)
  other arithmetic  12.3 us (4%)
  between operations  4.5 us (2%)
    unnamed x2, blocking collectives  112 us
    unnamed x28, local copies, waits for them, and re-layouts  50.5 us
    all_gather x1, blocking collectives, on_device(): gathered = lax.all_gather(stacked, 'vocab', axis=2, tiled=True)  33.2 us
    dot_general x1, matrix products, on_device(): jnp.dot(flat_spread, common_output_matrix, preferred_element_type=jnp.flo...  31.5 us
    psum x1, blocking collectives, on_device(): summed = lax.psum(jnp.sum(accepted).astype(jnp.float32), 'batch')  16.1 us
    all_to_all x1, blocking collectives, on_device(): lax.all_to_all(normed, 'batch', split_axis=2, concat_axis=0, tiled=True)  12.1 us
    all_to_all x1, local copies, waits for them, and re-layouts, on_device(): lax.all_to_all(normed, 'batch', split_axis=2, concat_axis=0, tiled=True)  12 us
    convert_element_type x1, local copies, waits for them, and re-layouts, on_device(): normed = (widened * lax.rsqrt(jnp.mean(widened * widened, -1, keepdims=Tr...  8.56 us
  transfers between devices with their start and end apart: 1, of which 0 were waited for; matrix products, arithmetic and copies ran while one was open for 1% of the time, Pallas kernels for 0%

commit v1 on v0

--- a/solution.py
+++ b/solution.py
@@ -1,6 +1,10 @@
+import functools
+
 import jax
 import jax.numpy as jnp
 from jax import lax
+from jax.experimental import pallas as pl
+from jax.experimental.pallas import tpu as pltpu
 from jax.sharding import PartitionSpec as P
 
 epsilon = 1e-05
@@ -105,9 +109,511 @@
     )
 
 
+MESH = pl.DeviceIdType.MESH
+lanes = 128
+
+
+def padded(count, tile):
+    return -(-count // tile) * tile
+
+
+def kernel(
+    shape,
+    softness_ref,
+    guess_ref,
+    early_ref,
+    deep_ref,
+    gain_ref,
+    draw_ref,
+    head_ref,
+    draft_lp_ref,
+    target_lp_ref,
+    draft_best_ref,
+    target_best_ref,
+    accepted_ref,
+    next_ref,
+    total_ref,
+    rows_f32,
+    square_mine,
+    square_in,
+    normed,
+    piece_in,
+    compact,
+    slot_mine,
+    slots,
+    x_ref,
+    part,
+    pair_in,
+    own,
+    cross_out,
+    cross_in,
+    soft_rows,
+    id_rows,
+    run_top,
+    run_total,
+    run_index,
+    run_picked,
+    stat_mine,
+    stat_in,
+    count_mine,
+    count_in,
+    square_send,
+    square_recv,
+    piece_send,
+    piece_recv,
+    slot_send,
+    slot_recv,
+    pair_send,
+    pair_recv,
+    cross_send,
+    cross_recv,
+    stat_send,
+    stat_recv,
+    count_send,
+    count_recv,
+):
+    vocab_size, batch_size, seqs, drafts, width, chunk, col_count, chunks = shape
+    positions = 2 * drafts + 1
+    used = seqs * positions
+    group = own.shape[1]
+    tall = rows_f32.shape[0]
+    block = rows_f32.shape[1]
+    piece = piece_in.shape[2]
+    share = vocab_size // batch_size
+    step = pl.program_id(0)
+    v = lax.axis_index("vocab")
+    b = lax.axis_index("batch")
+    low, high = lax.rem(b, 2), b // 2
+    pair_b = 2 * high + (1 - low)
+    cross_b = 2 * (1 - high) + low
+
+    def to_vocab(source, target, send, recv, d):
+        return pltpu.make_async_remote_copy(
+            src_ref=source,
+            dst_ref=target,
+            send_sem=send.at[d],
+            recv_sem=recv.at[d],
+            device_id=(lax.rem(v + d, vocab_size), b),
+            device_id_type=MESH,
+        )
+
+    def square_copy(d):
+        return to_vocab(square_mine, square_in.at[d], square_send, square_recv, d)
+
+    def slot_copy(d):
+        return to_vocab(slot_mine, slots.at[v], slot_send, slot_recv, d)
+
+    def stat_copy(d):
+        return to_vocab(stat_mine, stat_in.at[d], stat_send, stat_recv, d)
+
+    def count_copy(d):
+        return pltpu.make_async_remote_copy(
+            src_ref=count_mine,
+            dst_ref=count_in.at[d],
+            send_sem=count_send.at[d],
+            recv_sem=count_recv.at[d],
+            device_id=(v, lax.rem(b + d, batch_size)),
+            device_id_type=MESH,
+        )
+
+    def pair_copy(j):
+        return pltpu.make_async_remote_copy(
+            src_ref=part.at[j, pl.ds(pl.multiple_of((1 - low) * 2 * group, 8), 2 * group)],
+            dst_ref=pair_in.at[j],
+            send_sem=pair_send.at[j],
+            recv_sem=pair_recv.at[j],
+            device_id=(v, pair_b),
+            device_id_type=MESH,
+        )
+
+    def cross_copy(j):
+        return pltpu.make_async_remote_copy(
+            src_ref=cross_out.at[j],
+            dst_ref=cross_in.at[j],
+            send_sem=cross_send.at[j],
+            recv_sem=cross_recv.at[j],
+            device_id=(v, cross_b),
+            device_id_type=MESH,
+        )
+
+    home_b = v // share
+    home_v = batch_size * lax.rem(v, share)
+
+    def piece_copy(k):
+        return pltpu.make_async_remote_copy(
+            src_ref=normed.at[:, pl.ds(k * piece, piece)],
+            dst_ref=piece_in.at[b],
+            send_sem=piece_send.at[k],
+            recv_sem=piece_recv.at[b],
+            device_id=(home_v + k, home_b),
+            device_id_type=MESH,
+        )
+
+    def piece_local(k):
+        return pltpu.make_async_copy(
+            normed.at[:, pl.ds(k * piece, piece)], piece_in.at[b], piece_recv.at[b]
+        )
+
+    def piece_stays(k):
+        return (home_b == b) & (home_v + k == v)
+
+    def piece_arrival(other):
+        return pltpu.make_async_copy(
+            normed.at[:, pl.ds(0, piece)], piece_in.at[other], piece_recv.at[other]
+        )
+
+    @pl.when(step == 0)
+    def _():
+        barrier = pltpu.get_barrier_semaphore()
+        for d in range(1, vocab_size):
+            pl.semaphore_signal(
+                barrier, inc=1, device_id=(lax.rem(v + d, vocab_size), b), device_id_type=MESH
+            )
+        for d in range(1, batch_size):
+            pl.semaphore_signal(
+                barrier, inc=1, device_id=(v, lax.rem(b + d, batch_size)), device_id_type=MESH
+            )
+        origin_v = share * b + v // batch_size
+        for other in range(batch_size):
+
+            @pl.when((other != b) | (origin_v != v))
+            def _():
+                pl.semaphore_signal(
+                    barrier, inc=1, device_id=(origin_v, other), device_id_type=MESH
+                )
+
+        rows_f32[pl.ds(padded(used, 8) - 8, tall - padded(used, 8) + 8)] = jnp.zeros(
+            (tall - padded(used, 8) + 8, block), jnp.float32
+        )
+        deep = [deep_ref[p].astype(jnp.float32) for p in range(drafts + 1)]
+        for s in range(seqs):
+            start = s * positions
+            rows_f32[start : start + drafts] = early_ref[s].astype(jnp.float32)
+            for p in range(drafts + 1):
+                rows_f32[start + drafts + p : start + drafts + p + 1] = deep[p][s : s + 1]
+        rows = rows_f32[...]
+        squares = jnp.sum(rows * rows, -1, keepdims=True)
+        square_mine[...] = jnp.broadcast_to(squares, square_mine.shape)
+        stays = (home_b == b) & (v >= home_v) & (v < home_v + batch_size)
+        pl.semaphore_wait(
+            barrier, vocab_size - 1 + batch_size - 1 + batch_size - stays.astype(jnp.int32)
+        )
+        for d in range(1, vocab_size):
+            square_copy(d).start()
+        row = lax.broadcasted_iota(jnp.int32, soft_rows.shape, 0)
+        soft = jnp.full(soft_rows.shape, 1.0, jnp.float32)
+        ids = jnp.full(id_rows.shape, -1, jnp.int32)
+        for s in range(seqs):
+            start = s * positions
+            soft = jnp.where((row >= start) & (row < start + positions), softness_ref[s], soft)
+            for i in range(drafts):
+                hit = (row == start + i) | (row == start + drafts + i)
+                ids = jnp.where(hit, guess_ref[s, i], ids)
+        soft_rows[...] = soft
+        id_rows[...] = ids
+        gain = gain_ref[...].astype(jnp.float32)
+        total = square_mine[...]
+        for d in range(1, vocab_size):
+            square_copy(d).wait_recv()
+        for d in range(1, vocab_size):
+            total = total + square_in[d]
+        scale = lax.rsqrt(total[:, :1] / width + epsilon)
+        normed[...] = (rows_f32[...] * scale * gain).astype(jnp.bfloat16)
+        for k in range(batch_size):
+
+            @pl.when(piece_stays(k))
+            def _():
+                piece_local(k).start()
+
+            @pl.when(jnp.logical_not(piece_stays(k)))
+            def _():
+                piece_copy(k).start()
+
+        for other in range(batch_size):
+            piece_arrival(other).wait()
+        for other in range(batch_size):
+            place = ((other % 2) * 2 + other // 2) * group
+            compact[place : place + group] = piece_in[other].astype(jnp.float32)[:group]
+        mine = compact[...].astype(jnp.bfloat16)
+        slot_mine[...] = mine
+        for d in range(1, vocab_size):
+            slot_copy(d).start()
+        slots[v] = mine
+        for d in range(1, vocab_size):
+            pltpu.make_async_copy(
+                slot_mine, slots.at[lax.rem(v + vocab_size - d, vocab_size)], slot_recv.at[d]
+            ).wait()
+        for k in range(vocab_size):
+            x_ref[:, k * piece : (k + 1) * piece] = slots[k]
+
+    part[step] = lax.dot_general(
+        x_ref[...],
+        head_ref[...],
+        (((1,), (1,)), ((), ())),
+        preferred_element_type=jnp.float32,
+    )
+    pair_copy(step).start()
+
+    def join_pair(j):
+        pair_copy(j).wait_recv()
+        base = low * 2 * group
+        mine = pl.ds(pl.multiple_of(high * group, 8), group)
+        other = pl.ds(pl.multiple_of((1 - high) * group, 8), group)
+        mine_part = pl.ds(pl.multiple_of(base + high * group, 8), group)
+        other_part = pl.ds(pl.multiple_of(base + (1 - high) * group, 8), group)
+        cross_out[j] = part[j, other_part] + pair_in[j, other]
+        cross_copy(j).start()
+        own[j] = part[j, mine_part] + pair_in[j, mine]
+
+    @pl.when(step > 0)
+    def _():
+        join_pair(step - 1)
+
+    @pl.when(step == chunks - 1)
+    def _():
+        join_pair(chunks - 1)
+        run_top[...] = jnp.full(run_top.shape, -jnp.inf, jnp.float32)
+        run_total[...] = jnp.zeros(run_total.shape, jnp.float32)
+        run_index[...] = jnp.zeros(run_index.shape, jnp.float32)
+        run_picked[...] = jnp.zeros(run_picked.shape, jnp.float32)
+
+        def lap(j, carry):
+            cross_copy(j).wait_recv()
+            logits = (own[j] + cross_in[j]) / soft_rows[...]
+            local = j * chunk + lax.broadcasted_iota(jnp.int32, logits.shape, 1)
+            inside = local < col_count
+            column = local + v * col_count
+            logits = jnp.where(inside, logits, -jnp.inf)
+            top = run_top[...]
+            new_top = jnp.maximum(top, logits)
+            run_total[...] = run_total[...] * jnp.exp(top - new_top) + jnp.exp(logits - new_top)
+            run_index[...] = jnp.where(logits > top, column.astype(jnp.float32), run_index[...])
+            run_picked[...] += jnp.where(inside & (column == id_rows[...]), logits, 0.0)
+            run_top[...] = new_top
+            return carry
+
+        lax.fori_loop(0, chunks, lap, 0)
+        tops = run_top[...]
+        top = jnp.max(tops, -1, keepdims=True)
+        total = jnp.sum(run_total[...] * jnp.exp(tops - top), -1, keepdims=True)
+        index = jnp.min(
+            jnp.where(tops == top, run_index[...], jnp.float32(3e38)), -1, keepdims=True
+        )
+        picked = jnp.sum(run_picked[...], -1, keepdims=True)
+        lane = lax.broadcasted_iota(jnp.int32, stat_mine.shape, 1)
+        stat_mine[...] = jnp.where(
+            lane == 0, top, jnp.where(lane == 1, total, jnp.where(lane == 2, index, picked))
+        )
+        for d in range(1, vocab_size):
+            stat_copy(d).start()
+        for d in range(1, vocab_size):
+            stat_copy(d).wait_recv()
+        stats = [stat_mine[...]] + [stat_in[d] for d in range(1, vocab_size)]
+        all_top = functools.reduce(jnp.maximum, [s[:, 0:1] for s in stats])
+        all_total = sum(s[:, 1:2] * jnp.exp(s[:, 0:1] - all_top) for s in stats)
+        all_index = functools.reduce(
+            jnp.minimum, [jnp.where(s[:, 0:1] == all_top, s[:, 2:3], 3e38) for s in stats]
+        )
+        all_picked = sum(s[:, 3:4] for s in stats)
+        logprob = all_picked - (all_top + jnp.log(all_total))
+
+        row = lax.broadcasted_iota(jnp.int32, (group, lanes), 0)
+        lane = lax.broadcasted_iota(jnp.int32, (group, lanes), 1)
+
+        def laid_out(column, first, count):
+            found = [
+                jnp.sum(
+                    jnp.where((row == s * positions + first + lane) & (lane < count), column, 0.0),
+                    0,
+                    keepdims=True,
+                )
+                for s in range(seqs)
+            ]
+            return jnp.concatenate(found, 0)
+
+        draft_lp = laid_out(logprob, 0, drafts)
+        target_lp = laid_out(logprob, drafts, drafts)
+        draft_best = laid_out(all_index, 0, drafts)
+        target_best = laid_out(all_index, drafts, drafts + 1)
+        draft_lp_ref[...] = draft_lp[:, :drafts]
+        target_lp_ref[...] = target_lp[:, :drafts]
+        draft_best_ref[...] = draft_best[:, :drafts].astype(jnp.int32)
+        target_best_ref[...] = target_best[:, : drafts + 1].astype(jnp.int32)
+        passing = draw_ref[...].astype(jnp.float32) * inverse_range < jnp.exp(
+            target_lp[:, :drafts] - draft_lp[:, :drafts]
+        )
+        place = lax.broadcasted_iota(jnp.int32, (seqs, drafts), 1).astype(jnp.float32)
+        accepted = jnp.min(
+            jnp.where(passing, jnp.float32(drafts), place), -1, keepdims=True
+        )
+        spot = lax.broadcasted_iota(jnp.int32, (seqs, lanes), 1).astype(jnp.float32)
+        following = jnp.sum(jnp.where(spot == accepted, target_best, 0.0), -1, keepdims=True)
+        accepted_ref[...] = accepted.astype(jnp.int32)
+        next_ref[...] = following.astype(jnp.int32)
+        count_mine[...] = jnp.broadcast_to(
+            jnp.sum(accepted, 0, keepdims=True), count_mine.shape
+        )
+        for d in range(1, batch_size):
+            count_copy(d).start()
+        for d in range(1, batch_size):
+            count_copy(d).wait_recv()
+        count = count_mine[...]
+        for d in range(1, batch_size):
+            count = count + count_in[d]
+        total_ref[...] = count[:1, :1].astype(jnp.int32)
+
+        for d in range(1, vocab_size):
+            square_copy(d).wait_send()
+            slot_copy(d).wait_send()
+            stat_copy(d).wait_send()
+        for d in range(1, batch_size):
+            count_copy(d).wait_send()
+        for k in range(batch_size):
+
+            @pl.when(jnp.logical_not(piece_stays(k)))
+            def _():
+                piece_copy(k).wait_send()
+
+        def drain(j, carry):
+            pair_copy(j).wait_send()
+            cross_copy(j).wait_send()
+            return carry
+
+        lax.fori_loop(0, chunks, drain, 0)
+
+
+def fits(vocab_size, batch_size, seqs, width, col_count):
+    return (
+        batch_size == 4
+        and vocab_size % batch_size == 0
+        and width % (batch_size * vocab_size * lanes) == 0
+        and col_count >= chunk_width
+    )
+
+
+chunk_width = 512
+
+
+def fused(
+    vocab_size,
+    batch_size,
+    early_depth_activity,
+    deepest_depth_activity,
+    closing_gain_vector,
+    common_output_matrix,
+    softness_factor,
+    guessed_symbol_list,
+    acceptance_draw_numerators,
+):
+    seqs, drafts, block = early_depth_activity.shape
+    depth, col_count = common_output_matrix.shape
+    width = depth * batch_size
+    chunk = chunk_width
+    chunks = pl.cdiv(col_count, chunk)
+    positions = 2 * drafts + 1
+    group = padded(seqs * positions, 8)
+    tall = padded(seqs * positions, 16)
+    rows = batch_size * group
+    piece = depth // vocab_size
+    gain = lax.dynamic_slice(
+        closing_gain_vector, (lax.axis_index("vocab") * block,), (block,)
+    ).reshape(1, block)
+    f32, bf16, i32 = jnp.float32, jnp.bfloat16, jnp.int32
+    vmem = pl.BlockSpec(memory_space=pltpu.VMEM)
+    smem = pl.BlockSpec(memory_space=pltpu.SMEM)
+    dma = pltpu.SemaphoreType.DMA
+    shape = (vocab_size, batch_size, seqs, drafts, width, chunk, col_count, chunks)
+    results = pl.pallas_call(
+        functools.partial(kernel, shape),
+        grid=(chunks,),
+        out_shape=[
+            jax.ShapeDtypeStruct((seqs, drafts), f32),
+            jax.ShapeDtypeStruct((seqs, drafts), f32),
+            jax.ShapeDtypeStruct((seqs, drafts), i32),
+            jax.ShapeDtypeStruct((seqs, drafts + 1), i32),
+            jax.ShapeDtypeStruct((seqs, 1), i32),
+            jax.ShapeDtypeStruct((seqs, 1), i32),
+            jax.ShapeDtypeStruct((1, 1), i32),
+        ],
+        in_specs=[smem, smem, vmem, vmem, vmem, vmem]
+        + [pl.BlockSpec((chunk, depth), lambda j: (j, 0))],
+        out_specs=[vmem] * 7,
+        scratch_shapes=[
+            pltpu.VMEM((tall, block), f32),
+            pltpu.VMEM((tall, lanes), f32),
+            pltpu.VMEM((vocab_size, tall, lanes), f32),
+            pltpu.VMEM((tall, block), bf16),
+            pltpu.VMEM((batch_size, tall, piece), bf16),
+            pltpu.VMEM((rows, piece), f32),
+            pltpu.VMEM((rows, piece), bf16),
+            pltpu.VMEM((vocab_size, rows, piece), bf16),
+            pltpu.VMEM((rows, depth), bf16),
+            pltpu.VMEM((chunks, rows, chunk), f32),
+            pltpu.VMEM((chunks, 2 * group, chunk), f32),
+            pltpu.VMEM((chunks, group, chunk), f32),
+            pltpu.VMEM((chunks, group, chunk), f32),
+            pltpu.VMEM((chunks, group, chunk), f32),
+            pltpu.VMEM((group, chunk), f32),
+            pltpu.VMEM((group, chunk), i32),
+            pltpu.VMEM((group, chunk), f32),
+            pltpu.VMEM((group, chunk), f32),
+            pltpu.VMEM((group, chunk), f32),
+            pltpu.VMEM((group, chunk), f32),
+            pltpu.VMEM((group, lanes), f32),
+            pltpu.VMEM((vocab_size, group, lanes), f32),
+            pltpu.VMEM((8, lanes), f32),
+            pltpu.VMEM((batch_size, 8, lanes), f32),
+            dma((vocab_size,)),
+            dma((vocab_size,)),
+            dma((batch_size,)),
+            dma((batch_size,)),
+            dma((vocab_size,)),
+            dma((vocab_size,)),
+            dma((chunks,)),
+            dma((chunks,)),
+            dma((chunks,)),
+            dma((chunks,)),
+            dma((vocab_size,)),
+            dma((vocab_size,)),
+            dma((batch_size,)),
+            dma((batch_size,)),
+        ],
+        compiler_params=pltpu.CompilerParams(
+            collective_id=0,
+            has_side_effects=True,
+            vmem_limit_bytes=56 * 2**20,
+            dimension_semantics=("arbitrary",),
+        ),
+        cost_estimate=pl.CostEstimate(
+            flops=2 * rows * depth * col_count,
+            bytes_accessed=2 * depth * col_count,
+            transcendentals=2 * group * col_count,
+        ),
+    )(
+        softness_factor,
+        guessed_symbol_list,
+        early_depth_activity,
+        deepest_depth_activity.transpose(1, 0, 2),
+        gain,
+        acceptance_draw_numerators,
+        common_output_matrix.T,
+    )
+    first = results[:4]
+    return (*first, results[4].reshape(seqs), results[5].reshape(seqs), results[6].reshape(()))
+
+
 def solution(mesh):
+    vocab_size, batch_size = mesh.shape["vocab"], mesh.shape["batch"]
+
+    def body(*arrays):
+        depth, col_count = arrays[3].shape
+        seqs = arrays[0].shape[0]
+        if fits(vocab_size, batch_size, seqs, depth * batch_size, col_count):
+            return fused(vocab_size, batch_size, *arrays)
+        return on_device(*arrays)
+
     return jax.shard_map(
-        on_device,
+        body,
         mesh=mesh,
         in_specs=(
             P("batch", None, "vocab"),

time: 298 us -> 117 us (0.39)
  blocking collectives: 174 us -> 0 us
  Pallas kernels: 0 us -> 105 us
  local copies, waits for them, and re-layouts: 72.1 us -> 6.24 us
  matrix products: 31.5 us -> 0 us
  other arithmetic: 12.3 us -> 2.6 us
    unnamed x2 -> x0, blocking collectives: 112 us -> none
    pallas_call x0 -> x1, Pallas kernels: none -> 105 us  [fused(): pl.pallas_call(functools.partial(kernel, shape), grid=(chunks,), out_shap...]
    unnamed x28 -> x4, local copies, waits for them, and re-layouts: 50.5 us -> 4.96 us
    all_gather x1 -> x0, blocking collectives: 33.2 us -> none  [on_device(): gathered = lax.all_gather(stacked, 'vocab', axis=2, tiled=True)]
    dot_general x1 -> x0, matrix products: 31.5 us -> none  [on_device(): jnp.dot(flat_spread, common_output_matrix, preferred_element_type=jnp.flo...]
    psum x1 -> x0, blocking collectives: 16.1 us -> none  [on_device(): summed = lax.psum(jnp.sum(accepted).astype(jnp.float32), 'batch')]
    all_to_all x1 -> x0, blocking collectives: 12.1 us -> none  [on_device(): lax.all_to_all(normed, 'batch', split_axis=2, concat_axis=0, tiled=True)]
    all_to_all x1 -> x0, local copies, waits for them, and re-layouts: 12 us -> none  [on_device(): lax.all_to_all(normed, 'batch', split_axis=2, concat_axis=0, tiled=True)]
  transfers between devices with their start and end apart: 1 -> 0, of which waited for: 0 -> 0; matrix products, arithmetic and copies ran while one was open for 1% -> 0% of each run, Pallas kernels for 0% -> 0%
where the time goes in v1:
time: 117 us; the launch traced here: 116 us
  Pallas kernels  105 us (90%)
  local copies, waits for them, and re-layouts  6.24 us (5%)
  other arithmetic  2.6 us (2%)
  between operations  2.47 us (2%)
    pallas_call x1, Pallas kernels, fused(): pl.pallas_call(functools.partial(kernel, shape), grid=(chunks,), out_shap...  105 us
    unnamed x4, local copies, waits for them, and re-layouts  4.96 us
    pallas_call x2, other arithmetic, fused(): pl.pallas_call(functools.partial(kernel, shape), grid=(chunks,), out_shap...  2.6 us

profile of v1, /device:TPU:0, one launch (start us, length us, event | category | flops | bytes accessed | tf_op | source)
XLA Modules:
  0.0 116.1 jit_solution(16342833966503428505)
XLA Ops:
  0.6 0.7 dynamic_slice.3
  1.3 0.6 reshape.26.gain_ref
  1.9 104.8 %shard_map.126 = (f32[4,4]{1,0:T(4,128)}, f32[4,4]{1,0:T(4,128)}, s32[4,4]{1,0:T(4,128)}, s32[4,5]{1,0:T(4,128)}, s32[4,1]{1,0:T(4,128)}, /*index=5*/s32[4,1]{1,0:T(4,128)}, s32[1,1]{1,0:T(1,128)}) custom-call(f32[4]{0:T(128)} %softness_ref.1, s32[4,4]{1,0:T(4,128)} %guess_ref.1, bf16[4,4,1024]{2,1,0:T(4,128)(2,1)} %early_ref.1, ...), custom_call_target="tpu_custom_call" | custom-call | flops 10506731520 | bytes 65667072 | tf_op jit(solution)/shard_map/pallas_call | solution.py:526
  106.7 1.3 %reduce = s32[4]{0:T(128)} reduce(s32[4,1]{1,0:T(4,128)} %get-tuple-element.18, s32[]{:T(128)} %constant.10.clone.1), dimensions={1}, to_apply=%get-tuple-element.18.reduce_sub_computation | reduce | bytes 36 | tf_op jit(solution)/shard_map/pallas_call | solution.py:526
  108.0 1.3 %reduce.1 = s32[4]{0:T(128)} reduce(s32[4,1]{1,0:T(4,128)} %get-tuple-element.19, s32[]{:T(128)} %constant.10.clone.1), dimensions={1}, to_apply=%get-tuple-element.19.reduce_sub_computation | reduce | bytes 36 | tf_op jit(solution)/shard_map/pallas_call | solution.py:526
  109.3 1.2 %copy.19 = f32[4,4]{1,0:T(4,128)} copy(f32[4,4]{1,0:T(4,128)} %get-tuple-element.28) | data formatting | bytes 128
  110.6 1.2 %copy.20 = f32[4,4]{1,0:T(4,128)} copy(f32[4,4]{1,0:T(4,128)} %get-tuple-element.29) | data formatting | bytes 128
  111.8 1.2 %copy.21 = s32[4,4]{1,0:T(4,128)} copy(s32[4,4]{1,0:T(4,128)} %get-tuple-element.30) | data formatting | bytes 128
  113.1 1.2 %copy.22 = s32[4,5]{1,0:T(4,128)} copy(s32[4,5]{1,0:T(4,128)} %get-tuple-element.31) | data formatting | bytes 160

commit v2 on v1

--- a/solution.py
+++ b/solution.py
@@ -126,13 +126,8 @@
     gain_ref,
     draw_ref,
     head_ref,
-    draft_lp_ref,
-    target_lp_ref,
-    draft_best_ref,
-    target_best_ref,
-    accepted_ref,
-    next_ref,
-    total_ref,
+    table_ref,
+    count_ref,
     rows_f32,
     square_mine,
     square_in,
@@ -163,6 +158,8 @@
     piece_recv,
     slot_send,
     slot_recv,
+    along_send,
+    along_recv,
     pair_send,
     pair_recv,
     cross_send,
@@ -175,7 +172,8 @@
     vocab_size, batch_size, seqs, drafts, width, chunk, col_count, chunks = shape
     positions = 2 * drafts + 1
     used = seqs * positions
-    group = own.shape[1]
+    group = stat_mine.shape[0]
+    half = chunk // 2
     tall = rows_f32.shape[0]
     block = rows_f32.shape[1]
     piece = piece_in.shape[2]
@@ -203,6 +201,19 @@
     def slot_copy(d):
         return to_vocab(slot_mine, slots.at[v], slot_send, slot_recv, d)
 
+    beside = 2 * (v // 2) + 1 - lax.rem(v, 2)
+
+    def along_copy(d):
+        origin = lax.rem(v + vocab_size - d, vocab_size)
+        return pltpu.make_async_remote_copy(
+            src_ref=slot_mine if d == 0 else slots.at[origin],
+            dst_ref=slots.at[origin],
+            send_sem=along_send.at[d],
+            recv_sem=along_recv.at[d],
+            device_id=(beside, b),
+            device_id_type=MESH,
+        )
+
     def stat_copy(d):
         return to_vocab(stat_mine, stat_in.at[d], stat_send, stat_recv, d)
 
@@ -218,7 +229,7 @@
 
     def pair_copy(j):
         return pltpu.make_async_remote_copy(
-            src_ref=part.at[j, pl.ds(pl.multiple_of((1 - low) * 2 * group, 8), 2 * group)],
+            src_ref=part.at[j, pl.ds(pl.multiple_of((1 - low) * 2 * used, 8), 2 * used)],
             dst_ref=pair_in.at[j],
             send_sem=pair_send.at[j],
             recv_sem=pair_recv.at[j],
@@ -301,6 +312,7 @@
         for d in range(1, vocab_size):
             square_copy(d).start()
         row = lax.broadcasted_iota(jnp.int32, soft_rows.shape, 0)
+        row = jnp.where(row >= used, row - used, row)
         soft = jnp.full(soft_rows.shape, 1.0, jnp.float32)
         ids = jnp.full(id_rows.shape, -1, jnp.int32)
         for s in range(seqs):
@@ -332,17 +344,21 @@
         for other in range(batch_size):
             piece_arrival(other).wait()
         for other in range(batch_size):
-            place = ((other % 2) * 2 + other // 2) * group
-            compact[place : place + group] = piece_in[other].astype(jnp.float32)[:group]
+            place = ((other % 2) * 2 + other // 2) * used
+            compact[place : place + used] = piece_in[other].astype(jnp.float32)[:used]
         mine = compact[...].astype(jnp.bfloat16)
         slot_mine[...] = mine
-        for d in range(1, vocab_size):
+        for d in range(2, vocab_size, 2):
             slot_copy(d).start()
+        along_copy(0).start()
         slots[v] = mine
-        for d in range(1, vocab_size):
-            pltpu.make_async_copy(
-                slot_mine, slots.at[lax.rem(v + vocab_size - d, vocab_size)], slot_recv.at[d]
-            ).wait()
+        for d in sorted(range(2, vocab_size, 2), key=lambda d: min(d, vocab_size - d)):
+            origin = lax.rem(v + vocab_size - d, vocab_size)
+            pltpu.make_async_copy(slot_mine, slots.at[origin], slot_recv.at[d]).wait()
+            along_copy(d).start()
+        for d in range(0, vocab_size, 2):
+            origin = lax.rem(beside + vocab_size - d, vocab_size)
+            pltpu.make_async_copy(slot_mine, slots.at[origin], along_recv.at[d]).wait()
         for k in range(vocab_size):
             x_ref[:, k * piece : (k + 1) * piece] = slots[k]
 
@@ -356,22 +372,24 @@
 
     def join_pair(j):
         pair_copy(j).wait_recv()
-        base = low * 2 * group
-        mine = pl.ds(pl.multiple_of(high * group, 8), group)
-        other = pl.ds(pl.multiple_of((1 - high) * group, 8), group)
-        mine_part = pl.ds(pl.multiple_of(base + high * group, 8), group)
-        other_part = pl.ds(pl.multiple_of(base + (1 - high) * group, 8), group)
-        cross_out[j] = part[j, other_part] + pair_in[j, other]
+        pair = part[j, pl.ds(pl.multiple_of(low * 2 * used, 8), 2 * used)] + pair_in[j]
+        first, second = pair[:used], pair[used:]
+        away = jnp.where(high == 0, second, first)
+        cross_out[j, :used] = away[:, :half]
+        cross_out[j, used:] = away[:, half:]
         cross_copy(j).start()
-        own[j] = part[j, mine_part] + pair_in[j, mine]
-
-    @pl.when(step > 0)
+        stay = jnp.where(high == 0, first, second)
+        own[j, :used] = stay[:, :half]
+        own[j, used:] = stay[:, half:]
+
+    @pl.when(step > 1)
     def _():
-        join_pair(step - 1)
+        join_pair(step - 2)
 
     @pl.when(step == chunks - 1)
     def _():
-        join_pair(chunks - 1)
+        for j in range(max(chunks - 2, 0), chunks):
+            join_pair(j)
         run_top[...] = jnp.full(run_top.shape, -jnp.inf, jnp.float32)
         run_total[...] = jnp.zeros(run_total.shape, jnp.float32)
         run_index[...] = jnp.zeros(run_index.shape, jnp.float32)
@@ -380,7 +398,9 @@
         def lap(j, carry):
             cross_copy(j).wait_recv()
             logits = (own[j] + cross_in[j]) / soft_rows[...]
-            local = j * chunk + lax.broadcasted_iota(jnp.int32, logits.shape, 1)
+            row = lax.broadcasted_iota(jnp.int32, logits.shape, 0)
+            lane = lax.broadcasted_iota(jnp.int32, logits.shape, 1)
+            local = j * chunk + jnp.where(row >= used, lane + half, lane)
             inside = local < col_count
             column = local + v * col_count
             logits = jnp.where(inside, logits, -jnp.inf)
@@ -400,8 +420,19 @@
             jnp.where(tops == top, run_index[...], jnp.float32(3e38)), -1, keepdims=True
         )
         picked = jnp.sum(run_picked[...], -1, keepdims=True)
-        lane = lax.broadcasted_iota(jnp.int32, stat_mine.shape, 1)
-        stat_mine[...] = jnp.where(
+        tops, totals, indices = top, total, index
+        top = jnp.maximum(tops[:used], tops[used:])
+        total = totals[:used] * jnp.exp(tops[:used] - top) + totals[used:] * jnp.exp(
+            tops[used:] - top
+        )
+        index = jnp.minimum(
+            jnp.where(tops[:used] == top, indices[:used], jnp.float32(3e38)),
+            jnp.where(tops[used:] == top, indices[used:], jnp.float32(3e38)),
+        )
+        picked = picked[:used] + picked[used:]
+        stat_mine[...] = jnp.zeros(stat_mine.shape, jnp.float32)
+        lane = lax.broadcasted_iota(jnp.int32, (used, lanes), 1)
+        stat_mine[:used] = jnp.where(
             lane == 0, top, jnp.where(lane == 1, total, jnp.where(lane == 2, index, picked))
         )
         for d in range(1, vocab_size):
@@ -415,7 +446,8 @@
             jnp.minimum, [jnp.where(s[:, 0:1] == all_top, s[:, 2:3], 3e38) for s in stats]
         )
         all_picked = sum(s[:, 3:4] for s in stats)
-        logprob = all_picked - (all_top + jnp.log(all_total))
+        real = lax.broadcasted_iota(jnp.int32, all_total.shape, 0) < used
+        logprob = all_picked - (all_top + jnp.log(jnp.where(real, all_total, 1.0)))
 
         row = lax.broadcasted_iota(jnp.int32, (group, lanes), 0)
         lane = lax.broadcasted_iota(jnp.int32, (group, lanes), 1)
@@ -435,10 +467,10 @@
         target_lp = laid_out(logprob, drafts, drafts)
         draft_best = laid_out(all_index, 0, drafts)
         target_best = laid_out(all_index, drafts, drafts + 1)
-        draft_lp_ref[...] = draft_lp[:, :drafts]
-        target_lp_ref[...] = target_lp[:, :drafts]
-        draft_best_ref[...] = draft_best[:, :drafts].astype(jnp.int32)
-        target_best_ref[...] = target_best[:, : drafts + 1].astype(jnp.int32)
+        table_ref[0, :seqs] = draft_lp
+        table_ref[1, :seqs] = target_lp
+        table_ref[2, :seqs] = draft_best
+        table_ref[3, :seqs] = target_best
         passing = draw_ref[...].astype(jnp.float32) * inverse_range < jnp.exp(
             target_lp[:, :drafts] - draft_lp[:, :drafts]
         )
@@ -448,8 +480,6 @@
         )
         spot = lax.broadcasted_iota(jnp.int32, (seqs, lanes), 1).astype(jnp.float32)
         following = jnp.sum(jnp.where(spot == accepted, target_best, 0.0), -1, keepdims=True)
-        accepted_ref[...] = accepted.astype(jnp.int32)
-        next_ref[...] = following.astype(jnp.int32)
         count_mine[...] = jnp.broadcast_to(
             jnp.sum(accepted, 0, keepdims=True), count_mine.shape
         )
@@ -460,12 +490,18 @@
         count = count_mine[...]
         for d in range(1, batch_size):
             count = count + count_in[d]
-        total_ref[...] = count[:1, :1].astype(jnp.int32)
+        lane = lax.broadcasted_iota(jnp.int32, (seqs, lanes), 1)
+        count_ref[:seqs] = jnp.where(
+            lane == 0, accepted, jnp.where(lane == 1, following, count[:1])
+        ).astype(jnp.int32)
 
         for d in range(1, vocab_size):
             square_copy(d).wait_send()
-            slot_copy(d).wait_send()
             stat_copy(d).wait_send()
+        for d in range(0, vocab_size, 2):
+            along_copy(d).wait_send()
+            if d:
+                slot_copy(d).wait_send()
         for d in range(1, batch_size):
             count_copy(d).wait_send()
         for k in range(batch_size):
@@ -482,9 +518,33 @@
         lax.fori_loop(0, chunks, drain, 0)
 
 
-def fits(vocab_size, batch_size, seqs, width, col_count):
+def spread_out(
+    table_ref,
+    count_ref,
+    draft_lp_ref,
+    target_lp_ref,
+    draft_best_ref,
+    target_best_ref,
+    accepted_ref,
+    next_ref,
+    total_ref,
+):
+    seqs, drafts = draft_lp_ref.shape
+    draft_lp_ref[...] = table_ref[0, :seqs, :drafts]
+    target_lp_ref[...] = table_ref[1, :seqs, :drafts]
+    draft_best_ref[...] = table_ref[2, :seqs, :drafts].astype(jnp.int32)
+    target_best_ref[...] = table_ref[3, :seqs, : drafts + 1].astype(jnp.int32)
+    for s in range(seqs):
+        accepted_ref[s] = count_ref[s, 0]
+        next_ref[s] = count_ref[s, 1]
+    total_ref[0] = count_ref[0, 2]
+
+
+def fits(vocab_size, batch_size, seqs, positions, width, col_count):
     return (
         batch_size == 4
+        and seqs <= 8
+        and seqs * positions % 4 == 0
         and vocab_size % batch_size == 0
         and width % (batch_size * vocab_size * lanes) == 0
         and col_count >= chunk_width
@@ -513,7 +573,9 @@
     positions = 2 * drafts + 1
     group = padded(seqs * positions, 8)
     tall = padded(seqs * positions, 16)
-    rows = batch_size * group
+    used = seqs * positions
+    rows = batch_size * used
+    half = chunk // 2
     piece = depth // vocab_size
     gain = lax.dynamic_slice(
         closing_gain_vector, (lax.axis_index("vocab") * block,), (block,)
@@ -523,21 +585,16 @@
     smem = pl.BlockSpec(memory_space=pltpu.SMEM)
     dma = pltpu.SemaphoreType.DMA
     shape = (vocab_size, batch_size, seqs, drafts, width, chunk, col_count, chunks)
-    results = pl.pallas_call(
+    table, counts = pl.pallas_call(
         functools.partial(kernel, shape),
         grid=(chunks,),
         out_shape=[
-            jax.ShapeDtypeStruct((seqs, drafts), f32),
-            jax.ShapeDtypeStruct((seqs, drafts), f32),
-            jax.ShapeDtypeStruct((seqs, drafts), i32),
-            jax.ShapeDtypeStruct((seqs, drafts + 1), i32),
-            jax.ShapeDtypeStruct((seqs, 1), i32),
-            jax.ShapeDtypeStruct((seqs, 1), i32),
-            jax.ShapeDtypeStruct((1, 1), i32),
+            jax.ShapeDtypeStruct((4, 8, lanes), f32),
+            jax.ShapeDtypeStruct((8, lanes), i32),
         ],
         in_specs=[smem, smem, vmem, vmem, vmem, vmem]
         + [pl.BlockSpec((chunk, depth), lambda j: (j, 0))],
-        out_specs=[vmem] * 7,
+        out_specs=[vmem] * 2,
         scratch_shapes=[
             pltpu.VMEM((tall, block), f32),
             pltpu.VMEM((tall, lanes), f32),
@@ -549,16 +606,16 @@
             pltpu.VMEM((vocab_size, rows, piece), bf16),
             pltpu.VMEM((rows, depth), bf16),
             pltpu.VMEM((chunks, rows, chunk), f32),
-            pltpu.VMEM((chunks, 2 * group, chunk), f32),
-            pltpu.VMEM((chunks, group, chunk), f32),
-            pltpu.VMEM((chunks, group, chunk), f32),
-            pltpu.VMEM((chunks, group, chunk), f32),
-            pltpu.VMEM((group, chunk), f32),
-            pltpu.VMEM((group, chunk), i32),
-            pltpu.VMEM((group, chunk), f32),
-            pltpu.VMEM((group, chunk), f32),
-            pltpu.VMEM((group, chunk), f32),
-            pltpu.VMEM((group, chunk), f32),
+            pltpu.VMEM((chunks, 2 * used, chunk), f32),
+            pltpu.VMEM((chunks, 2 * used, half), f32),
+            pltpu.VMEM((chunks, 2 * used, half), f32),
+            pltpu.VMEM((chunks, 2 * used, half), f32),
+            pltpu.VMEM((2 * used, half), f32),
+            pltpu.VMEM((2 * used, half), i32),
+            pltpu.VMEM((2 * used, half), f32),
+            pltpu.VMEM((2 * used, half), f32),
+            pltpu.VMEM((2 * used, half), f32),
+            pltpu.VMEM((2 * used, half), f32),
             pltpu.VMEM((group, lanes), f32),
             pltpu.VMEM((vocab_size, group, lanes), f32),
             pltpu.VMEM((8, lanes), f32),
@@ -567,6 +624,8 @@
             dma((vocab_size,)),
             dma((batch_size,)),
             dma((batch_size,)),
+            dma((vocab_size,)),
+            dma((vocab_size,)),
             dma((vocab_size,)),
             dma((vocab_size,)),
             dma((chunks,)),
@@ -598,8 +657,21 @@
         acceptance_draw_numerators,
         common_output_matrix.T,
     )
-    first = results[:4]
-    return (*first, results[4].reshape(seqs), results[5].reshape(seqs), results[6].reshape(()))
+    results = pl.pallas_call(
+        spread_out,
+        out_shape=[
+            jax.ShapeDtypeStruct((seqs, drafts), f32),
+            jax.ShapeDtypeStruct((seqs, drafts), f32),
+            jax.ShapeDtypeStruct((seqs, drafts), i32),
+            jax.ShapeDtypeStruct((seqs, drafts + 1), i32),
+            jax.ShapeDtypeStruct((seqs,), i32),
+            jax.ShapeDtypeStruct((seqs,), i32),
+            jax.ShapeDtypeStruct((1,), i32),
+        ],
+        in_specs=[vmem, smem],
+        out_specs=[vmem] * 4 + [smem] * 3,
+    )(table, counts)
+    return (*results[:6], results[6].reshape(()))
 
 
 def solution(mesh):
@@ -607,8 +679,8 @@
 
     def body(*arrays):
         depth, col_count = arrays[3].shape
-        seqs = arrays[0].shape[0]
-        if fits(vocab_size, batch_size, seqs, depth * batch_size, col_count):
+        seqs, drafts = arrays[0].shape[:2]
+        if fits(vocab_size, batch_size, seqs, 2 * drafts + 1, depth * batch_size, col_count):
             return fused(vocab_size, batch_size, *arrays)
         return on_device(*arrays)
 

time: 117 us -> 101 us (0.86)
  Pallas kernels: 105 us -> 98 us
  local copies, waits for them, and re-layouts: 6.24 us -> 1.28 us
  other arithmetic: 2.6 us -> 0 us
  between operations: 2.47 us -> 0.65 us
    pallas_call x1, Pallas kernels: 105 us -> 96.6 us  [fused(): pl.pallas_call(functools.partial(kernel, shape), grid=(chunks,), out_shap...]
    unnamed x4 -> x0, local copies, waits for them, and re-layouts: 4.96 us -> none
    pallas_call x2 -> x0, other arithmetic: 2.6 us -> none  [fused(): pl.pallas_call(functools.partial(kernel, shape), grid=(chunks,), out_shap...]
    pallas_call x0 -> x1, Pallas kernels: none -> 1.46 us  [fused(): pl.pallas_call(spread_out, out_shape=[jax.ShapeDtypeStruct((seqs, drafts)...]
where the time goes in v2:
time: 101 us; the launch traced here: 100 us
  Pallas kernels  98 us (97%)
  local copies, waits for them, and re-layouts  1.28 us (1%)
    pallas_call x1, Pallas kernels, fused(): pl.pallas_call(functools.partial(kernel, shape), grid=(chunks,), out_shap...  96.6 us

profile of v2, /device:TPU:0, one launch (start us, length us, event | category | flops | bytes accessed | tf_op | source)
XLA Modules:
  0.0 100.0 jit_solution(8232378229219288922)
XLA Ops:
  0.6 0.7 dynamic_slice.3
  1.3 0.6 reshape.20.gain_ref
  1.9 96.6 %shard_map.126 = (f32[4,8,128]{2,1,0:T(8,128)}, s32[8,128]{1,0:T(8,128)}) custom-call(f32[4]{0:T(128)} %softness_ref.1, s32[4,4]{1,0:T(4,128)} %guess_ref.1, bf16[4,4,1024]{2,1,0:T(4,128)(2,1)} %early_ref.1, bf16[5,4,1024]{2,1,0:T(4,128)(2,1)} %bitcast.4, bf16[1,1024]{1,0:T(2,128)(2,1)} %reshape.20.gain_ref, s32[4,4]{1,0:T(4,128)} %draw_ref.1, ...), custom_call_target="tpu_custom_call" | custom-call | flops 9456058368 | bytes 65667072 | tf_op jit(solution)/shard_map/pallas_call | solution.py:588
  98.5 1.5 %shard_map.127 = (f32[4,4]{1,0:T(4,128)}, f32[4,4]{1,0:T(4,128)}, s32[4,4]{1,0:T(4,128)}, s32[4,5]{1,0:T(4,128)}, s32[4]{0:T(128)}, /*index=5*/s32[4]{0:T(128)}, s32[1]{0:T(128)}) custom-call(f32[4,8,128]{2,1,0:T(8,128)} %get-tuple-element.16.table_ref, s32[8,128]{1,0:T(8,128)} %get-tuple-element.17.count_ref), custom_call_target="tpu_custom_call" | custom-call | tf_op jit(solution)/shard_map/pallas_call | solution.py:660

commit v3 on v2

--- a/solution.py
+++ b/solution.py
@@ -131,11 +131,15 @@
     rows_f32,
     square_mine,
     square_in,
+    scale_mine,
+    scale_in,
+    scale_rows,
     normed,
     piece_in,
     compact,
     slot_mine,
     slots,
+    wide,
     x_ref,
     part,
     pair_in,
@@ -154,6 +158,8 @@
     count_in,
     square_send,
     square_recv,
+    scale_send,
+    scale_recv,
     piece_send,
     piece_recv,
     slot_send,
@@ -176,6 +182,7 @@
     half = chunk // 2
     tall = rows_f32.shape[0]
     block = rows_f32.shape[1]
+    rows_count = compact.shape[0]
     piece = piece_in.shape[2]
     share = vocab_size // batch_size
     step = pl.program_id(0)
@@ -223,6 +230,16 @@
             dst_ref=count_in.at[d],
             send_sem=count_send.at[d],
             recv_sem=count_recv.at[d],
+            device_id=(v, lax.rem(b + d, batch_size)),
+            device_id_type=MESH,
+        )
+
+    def scale_copy(d):
+        return pltpu.make_async_remote_copy(
+            src_ref=scale_mine,
+            dst_ref=scale_in.at[b],
+            send_sem=scale_send.at[d],
+            recv_sem=scale_recv.at[d],
             device_id=(v, lax.rem(b + d, batch_size)),
             device_id_type=MESH,
         )
@@ -311,6 +328,17 @@
         )
         for d in range(1, vocab_size):
             square_copy(d).start()
+        normed[...] = rows.astype(jnp.bfloat16)
+        for k in range(batch_size):
+
+            @pl.when(piece_stays(k))
+            def _():
+                piece_local(k).start()
+
+            @pl.when(jnp.logical_not(piece_stays(k)))
+            def _():
+                piece_copy(k).start()
+
         row = lax.broadcasted_iota(jnp.int32, soft_rows.shape, 0)
         row = jnp.where(row >= used, row - used, row)
         soft = jnp.full(soft_rows.shape, 1.0, jnp.float32)
@@ -323,24 +351,17 @@
                 ids = jnp.where(hit, guess_ref[s, i], ids)
         soft_rows[...] = soft
         id_rows[...] = ids
-        gain = gain_ref[...].astype(jnp.float32)
+        wide[rows_count:] = jnp.zeros((wide.shape[0] - rows_count, piece), jnp.float32)
         total = square_mine[...]
         for d in range(1, vocab_size):
             square_copy(d).wait_recv()
         for d in range(1, vocab_size):
             total = total + square_in[d]
-        scale = lax.rsqrt(total[:, :1] / width + epsilon)
-        normed[...] = (rows_f32[...] * scale * gain).astype(jnp.bfloat16)
-        for k in range(batch_size):
-
-            @pl.when(piece_stays(k))
-            def _():
-                piece_local(k).start()
-
-            @pl.when(jnp.logical_not(piece_stays(k)))
-            def _():
-                piece_copy(k).start()
-
+        scale = lax.rsqrt(total / width + epsilon)
+        scale_mine[...] = scale
+        scale_in[b] = scale
+        for d in range(1, batch_size):
+            scale_copy(d).start()
         for other in range(batch_size):
             piece_arrival(other).wait()
         for other in range(batch_size):
@@ -359,15 +380,22 @@
         for d in range(0, vocab_size, 2):
             origin = lax.rem(beside + vocab_size - d, vocab_size)
             pltpu.make_async_copy(slot_mine, slots.at[origin], along_recv.at[d]).wait()
+        for d in range(1, batch_size):
+            pltpu.make_async_copy(
+                scale_mine, scale_in.at[lax.rem(b + batch_size - d, batch_size)], scale_recv.at[d]
+            ).wait()
+        for other in range(batch_size):
+            place = ((other % 2) * 2 + other // 2) * used
+            scale_rows[place : place + used] = scale_in[other][:used]
+        scale = scale_rows[:, :1]
+        gain = gain_ref[...].astype(jnp.float32)
         for k in range(vocab_size):
-            x_ref[:, k * piece : (k + 1) * piece] = slots[k]
-
-    part[step] = lax.dot_general(
-        x_ref[...],
-        head_ref[...],
-        (((1,), (1,)), ((), ())),
-        preferred_element_type=jnp.float32,
-    )
+            cut = slice(k * piece, (k + 1) * piece)
+            wide[:rows_count] = slots[k].astype(jnp.float32) * scale * gain[:, cut]
+            x_ref[cut, :] = wide[...].T.astype(jnp.bfloat16)
+
+    product = jnp.dot(head_ref[...], x_ref[...], preferred_element_type=jnp.float32)
+    part[step] = product.T[:rows_count]
     pair_copy(step).start()
 
     def join_pair(j):
@@ -503,6 +531,7 @@
             if d:
                 slot_copy(d).wait_send()
         for d in range(1, batch_size):
+            scale_copy(d).wait_send()
             count_copy(d).wait_send()
         for k in range(batch_size):
 
@@ -551,7 +580,7 @@
     )
 
 
-chunk_width = 512
+chunk_width = 1024
 
 
 def fused(
@@ -578,8 +607,8 @@
     half = chunk // 2
     piece = depth // vocab_size
     gain = lax.dynamic_slice(
-        closing_gain_vector, (lax.axis_index("vocab") * block,), (block,)
-    ).reshape(1, block)
+        closing_gain_vector, (lax.axis_index("batch") * depth,), (depth,)
+    ).reshape(1, depth)
     f32, bf16, i32 = jnp.float32, jnp.bfloat16, jnp.int32
     vmem = pl.BlockSpec(memory_space=pltpu.VMEM)
     smem = pl.BlockSpec(memory_space=pltpu.SMEM)
@@ -599,12 +628,16 @@
             pltpu.VMEM((tall, block), f32),
             pltpu.VMEM((tall, lanes), f32),
             pltpu.VMEM((vocab_size, tall, lanes), f32),
+            pltpu.VMEM((tall, lanes), f32),
+            pltpu.VMEM((batch_size, tall, lanes), f32),
+            pltpu.VMEM((rows, lanes), f32),
             pltpu.VMEM((tall, block), bf16),
             pltpu.VMEM((batch_size, tall, piece), bf16),
             pltpu.VMEM((rows, piece), f32),
             pltpu.VMEM((rows, piece), bf16),
             pltpu.VMEM((vocab_size, rows, piece), bf16),
-            pltpu.VMEM((rows, depth), bf16),
+            pltpu.VMEM((padded(rows, lanes), piece), f32),
+            pltpu.VMEM((depth, padded(rows, lanes)), bf16),
             pltpu.VMEM((chunks, rows, chunk), f32),
             pltpu.VMEM((chunks, 2 * used, chunk), f32),
             pltpu.VMEM((chunks, 2 * used, half), f32),
@@ -622,6 +655,8 @@
             pltpu.VMEM((batch_size, 8, lanes), f32),
             dma((vocab_size,)),
             dma((vocab_size,)),
+            dma((batch_size,)),
+            dma((batch_size,)),
             dma((batch_size,)),
             dma((batch_size,)),
             dma((vocab_size,)),

time: 101 us -> 100 us (0.990)
  no operation moved by 1% of the time
where the time goes in v3:
time: 100 us; the launch traced here: 99.9 us
  Pallas kernels  97.9 us (98%)
  local copies, waits for them, and re-layouts  1.3 us (1%)
    pallas_call x1, Pallas kernels, fused(): pl.pallas_call(functools.partial(kernel, shape), grid=(chunks,), out_shap...  96.5 us

profile of v3, /device:TPU:0, one launch (start us, length us, event | category | flops | bytes accessed | tf_op | source)
XLA Modules:
  0.0 99.9 jit_solution(12663366663300153069)
XLA Ops:
  0.6 0.7 dynamic_slice.3
  1.3 0.6 reshape.20.gain_ref
  1.9 96.5 %shard_map.126 = (f32[4,8,128]{2,1,0:T(8,128)}, s32[8,128]{1,0:T(8,128)}) custom-call(f32[4]{0:T(128)} %softness_ref.1, s32[4,4]{1,0:T(4,128)} %guess_ref.1, bf16[4,4,1024]{2,1,0:T(4,128)(2,1)} %early_ref.1, bf16[5,4,1024]{2,1,0:T(4,128)(2,1)} %bitcast.4, bf16[1,2048]{1,0:T(2,128)(2,1)} %reshape.20.gain_ref, s32[4,4]{1,0:T(4,128)} %draw_ref.1, ...), custom_call_target="tpu_custom_call" | custom-call | flops 9456058368 | bytes 65667072 | tf_op jit(solution)/shard_map/pallas_call | solution.py:617
  98.4 1.5 %shard_map.127 = (f32[4,4]{1,0:T(4,128)}, f32[4,4]{1,0:T(4,128)}, s32[4,4]{1,0:T(4,128)}, s32[4,5]{1,0:T(4,128)}, s32[4]{0:T(128)}, /*index=5*/s32[4]{0:T(128)}, s32[1]{0:T(128)}) custom-call(f32[4,8,128]{2,1,0:T(8,128)} %get-tuple-element.16.table_ref, s32[8,128]{1,0:T(8,128)} %get-tuple-element.17.count_ref), custom_call_target="tpu_custom_call" | custom-call | tf_op jit(solution)/shard_map/pallas_call | solution.py:695
